TPU v7x, 128 devices: a whole 4x4x4 slice. The times are simulated.
128 devices in a mesh: month: 4 (over x_hi, core), mascon: 32 (over z, y, x_lo).
Axes of the slice: x: 4 (x_hi: 2, x_lo: 2; x = x_hi * 2 + x_lo), y: 4, z: 4, core: 2. Of those that a mesh axis runs over, the one named last changes fastest.
Arguments:
- panels: bfloat16 [32, 128, 40960], P('month', None, 'mascon'), may hold values from -0.0546875 to 0.0546875
- observations: bfloat16 [32, 128, 256], P('month'), may hold values from -6 to 6
- data_weights: bfloat16 [32, 128], P('month'), may hold values from 0.25 to 2
- arc_month: int32 [32], replicated, may hold values from 0 to 3, as said below
- fields: float32 [4, 40960, 256], P('month', 'mascon'), may hold values from -6 to 6
- diag_scale: float32 [4, 40960], P('month', 'mascon'), may hold values from 1.5 to 6
- smooth_coef: float32 [6, 40960], P(None, 'mascon'), may hold values from 0.05 to 0.5
- neighbours: int32 [6, 40960], P(None, 'mascon'), may hold values from 0 to 40959, as said below
- time_coupling: float32 [40960], P('mascon'), may hold values from 0.1 to 1
Outputs:
- solution: float32 [4, 40960, 256], P('month', 'mascon')
Inputs may be any that keep to these rules, and one draw needn't show every extreme that they name: `arc_month`: within each aligned block of 8 arcs, at most 4 arcs have months in any one group of 1 consecutive months (months g * 1 to (g + 1) - 1); one such group receives exactly 4 arcs from every block. `neighbours`: each stencil neighbour lies within 64 positions of its mascon in the cyclic mascon order, and is never the mascon itself.
All inputs are finite; a program needn't handle non-finite values.
Results may differ from a plain program's by a relative error of at most 0.0009.
Values may be sent and summed in bfloat16 or wider, within the bound.
A program may use at most 128 MiB of HBM per device.

v0:
```python
import functools

import jax
import jax.numpy as jnp
from jax import lax
from jax.experimental import pallas as pl
from jax.experimental.pallas import tpu as pltpu
from jax.sharding import PartitionSpec as P

MESH = pl.DeviceIdType.MESH
HALO = 64
ITERS = 2
HALVES = 2
BLOCK = 128
CHUNKS = 2
LEVELS = 32767.0
RELAX = 0.5

PEERS = (10, 6, 9, 14, 11, 5, 15, 7, 13, 2, 8, 1, 4, 3, 12)

F32, BF16, I16 = jnp.float32, jnp.bfloat16, jnp.int16


def encode(x):
    top = jnp.maximum(jnp.max(jnp.abs(x), axis=0, keepdims=True), 1e-30)
    code = jnp.round(x * (LEVELS / top)).astype(jnp.int32).astype(I16)
    return code, top * (1.0 / LEVELS)


def decode(code, scale):
    return code.astype(jnp.int32).astype(F32) * scale


def kernel(
    shape,
    arc_month,
    panels_hbm,
    obs_hbm,
    weights_hbm,
    fields_hbm,
    diag_hbm,
    coef_hbm,
    neighbours_hbm,
    coupling_hbm,
    out_hbm,
    panels,
    obs,
    weights,
    diag,
    coef,
    neighbours,
    coupling,
    result,
    turned,
    wide,
    coded,
    scales,
    states,
    every_month,
    track,
    partial,
    lane_sum,
    lane_got,
    resid,
    masked,
    grad,
    grad_code,
    grad_scale,
    grad_code_in,
    grad_scale_in,
    base,
    weight_rows,
    stencil,
    keep_rows,
    step_rows,
    time_rows,
    columns,
    split,
    load_sem,
    store_sem,
    plane_send,
    plane_recv,
    one_send,
    one_recv,
    turn_sem,
):
    cols, arcs, rows, total = shape
    blocks = cols // BLOCK
    chunk = cols // CHUNKS
    chunk_blocks = chunk // BLOCK
    every = arcs * rows
    piece = every // 16
    g, s = lax.axis_index("month"), lax.axis_index("mascon")
    core, hi = g % 2, g // 2
    z, y, x_lo = s // 8, (s // 2) % 4, s % 2
    q = z * 4 + y
    mate_month = g + 1 - 2 * core
    pair_month = (g + 2) % 4
    far_month = (mate_month + 2) % 4
    mate = (mate_month, s)
    pair = (pair_month, s)
    beside = (g, s + 1 - 2 * x_lo)
    right = (g, (s + 1) % 32)
    left = (g, (s + 31) % 32)

    def peer(d):
        return ((z + d // 4) % 4) * 4 + (y + d % 4) % 4

    def device(p):
        return (g, p * 2 + x_lo)

    across = ("pc0", "ps0", "pc1", "ps1")
    local = ("mc", "ms")
    rims = ("hl", "hr")

    barrier = pltpu.get_barrier_semaphore()

    def greet(d, carry):
        pl.semaphore_signal(barrier, inc=1, device_id=device(peer(d)), device_id_type=MESH)
        return carry

    lax.fori_loop(1, 16, greet, 0)
    for other in (mate, pair, left, right):
        pl.semaphore_signal(barrier, inc=1, device_id=other, device_id_type=MESH)

    loads = [
        pltpu.make_async_copy(
            fields_hbm.at[0, :, pl.ds(h * BLOCK, BLOCK)], wide.at[0, h, pl.ds(HALO, cols)], load_sem.at[h]
        )
        for h in range(HALVES)
    ]
    pairs = (
        (panels_hbm, panels),
        (neighbours_hbm, neighbours),
        (coef_hbm, coef),
        (diag_hbm, diag),
        (coupling_hbm, coupling),
        (weights_hbm, weights),
        (obs_hbm, obs),
    )
    loads += [pltpu.make_async_copy(src, dst, load_sem.at[HALVES + i]) for i, (src, dst) in enumerate(pairs)]
    for load in loads:
        load.start()

    names = ("pc0", "pc1", "ps0", "ps1", "fc0", "fc1", "fs0", "fs1", "gc0", "gc1", "gs0", "gs1")
    names += ("mc", "ms", "hl", "hr", "xl", "wm")
    targets = (pair, pair, pair, pair, mate, mate, mate, mate, pair, pair, pair, pair)
    targets += (mate, mate, left, right, beside, mate)

    def copy(it, h, name):
        w = wide.at[it, h]
        c = int(name[2]) if len(name) == 3 else 0
        part = pl.ds(c * chunk, chunk)
        if name[:2] == "pc":
            src = dst = coded.at[it, h, g, part]
        elif name[:2] == "ps":
            src = dst = scales.at[it, h, g, c]
        elif name[:2] == "fc":
            src = dst = coded.at[it, h, pair_month, part]
        elif name[:2] == "fs":
            src = dst = scales.at[it, h, pair_month, c]
        elif name[:2] == "gc":
            src, dst = grad_code.at[it, h, part], grad_code_in.at[it, h, part]
        elif name[:2] == "gs":
            src, dst = grad_scale.at[it, h, c], grad_scale_in.at[it, h, c]
        elif name == "mc":
            src = dst = coded.at[it, h, g]
        elif name == "ms":
            src = dst = scales.at[it, h, g]
        elif name == "hl":
            src, dst = w.at[pl.ds(HALO, HALO)], w.at[pl.ds(HALO + cols, HALO)]
        elif name == "hr":
            src, dst = w.at[pl.ds(cols, HALO)], w.at[pl.ds(0, HALO)]
        elif name == "xl":
            src, dst = lane_sum.at[it, h], lane_got.at[it, h]
        else:
            src = dst = resid.at[it, h, core]
        i = names.index(name)
        return pltpu.make_async_remote_copy(
            src_ref=src,
            dst_ref=dst,
            send_sem=one_send.at[it * HALVES + h, i],
            recv_sem=one_recv.at[it * HALVES + h, i],
            device_id=targets[i],
            device_id_type=MESH,
        )

    waited = set()

    def sent(it, h, *which):
        for name in which:
            if (it, h, name) not in waited:
                waited.add((it, h, name))
                copy(it, h, name).wait_send()

    def start(it, h, *which):
        for name in which:
            copy(it, h, name).start()

    def arrived(it, h, *which):
        for name in which:
            copy(it, h, name).wait_recv()

    def plane(it, h, phase, d, src, dst):
        return pltpu.make_async_remote_copy(
            src_ref=src,
            dst_ref=dst,
            send_sem=plane_send.at[(it * HALVES + h) * 2 + phase, d],
            recv_sem=plane_recv.at[(it * HALVES + h) * 2 + phase, d],
            device_id=device(peer(d)),
            device_id_type=MESH,
        )

    def reduce_copy(it, h, d):
        first = pl.multiple_of(peer(d) * piece, piece)
        return plane(it, h, 0, d, track.at[it, h, pl.ds(first, piece)], partial.at[it, h, d])

    def gather_copy(it, h, d):
        first = pl.multiple_of(q * piece, piece)
        own = resid.at[it, h, core, pl.ds(first, piece)]
        return plane(it, h, 1, d, own, own)

    def loop(low, high, body):
        def run(i, carry):
            body(i)
            return carry

        lax.fori_loop(low, high, run, 0)

    def over_blocks(c, body):
        loop(0, chunk_blocks, lambda b: body(b, pl.multiple_of(c * chunk + b * BLOCK, BLOCK)))

    def lane(month):
        return pl.multiple_of((((month // 2) + hi) % 2 * 2 + month % 2) * BLOCK, BLOCK)

    def encode_state(it, h, c):
        def body(b, r):
            x = wide[it, h, pl.ds(HALO + r, BLOCK), :]
            code, scale = encode(x)
            coded[it, h, g, pl.ds(r, BLOCK), :] = code
            scales[it, h, g, c, pl.ds(b, 1), :] = scale
            states[h, pl.ds(r, BLOCK), pl.ds(lane(g), BLOCK)] = x.astype(BF16)

        over_blocks(c, body)

    def unpack(it, h, month, c):
        def body(b, r):
            x = decode(coded[it, h, month, pl.ds(r, BLOCK), :], scales[it, h, month, c, pl.ds(b, 1), :])
            states[h, pl.ds(r, BLOCK), pl.ds(lane(month), BLOCK)] = x.astype(BF16)

        over_blocks(c, body)

    def predict(h, side):
        def part(i):
            r = pl.multiple_of(i * (every // 2), every // 2)
            sums = jnp.dot(
                panels[pl.ds(r, every // 2), :],
                states[h, :, pl.ds(side * 2 * BLOCK, 2 * BLOCK)],
                preferred_element_type=F32,
            )
            every_month[side * 2, pl.ds(r, every // 2), :] = sums[:, :BLOCK]
            every_month[side * 2 + 1, pl.ds(r, every // 2), :] = sums[:, BLOCK:]

        loop(0, 2, part)

    def chip_months(it, h):
        arrived(it, h, "mc", "ms")
        for c in range(CHUNKS):
            unpack(it, h, mate_month, c)
        predict(h, 0)

    def far_arrive(it, h):
        for c in range(CHUNKS):
            arrived(it, h, f"pc{c}", f"ps{c}")
            start(it, h, f"fc{c}", f"fs{c}")
            unpack(it, h, pair_month, c)

    def far_predict(it, h):
        for c in range(CHUNKS):
            arrived(it, h, f"fc{c}", f"fs{c}")
            unpack(it, h, far_month, c)
        predict(h, 1)

        def choose(a):
            month = arc_month[g * arcs + a]
            r = pl.multiple_of(a * rows, rows)
            place = (month // 2 + hi) % 2 * 2 + month % 2
            track[it, h, pl.ds(r, rows), :] = every_month[place, pl.ds(r, rows), :]

        loop(0, arcs, choose)

    def reduce_start(it, h):
        for d in PEERS:
            reduce_copy(it, h, d).start()

    def reduce_plane(it, h):
        def add(d, acc):
            reduce_copy(it, h, d).wait_recv()
            return acc + partial[it, h, d]

        own = track[it, h, pl.ds(pl.multiple_of(q * piece, piece), piece), :]
        lane_sum[it, h] = lax.fori_loop(1, 16, add, own)
        start(it, h, "xl")

    def weigh(it, h):
        own = pl.ds(pl.multiple_of(q * piece, piece), piece)
        arrived(it, h, "xl")
        full = lane_sum[it, h] + lane_got[it, h]
        seen = obs[own, pl.ds(h * BLOCK, BLOCK)].astype(F32)
        resid[it, h, core, own, :] = (weight_rows[own, :] * (full - seen)).astype(BF16)
        for d in PEERS:
            gather_copy(it, h, d).start()

    def place_resid(it, h, blk):
        def arc(a):
            month = arc_month[(hi * 2 + blk) * arcs + a]
            r = pl.multiple_of(a * rows, rows)
            w = resid[it, h, blk, pl.ds(r, rows), :].astype(F32)
            masked[blk, pl.ds(r, rows), pl.ds(0, BLOCK)] = jnp.where(month == pair_month, w, 0.0).astype(BF16)
            masked[blk, pl.ds(r, rows), pl.ds(BLOCK, BLOCK)] = jnp.where(month == g, w, 0.0).astype(BF16)

        loop(0, arcs, arc)

    def gradient_here(it, h):
        loop(1, 16, lambda d: gather_copy(it, h, d).wait_recv())
        start(it, h, "wm")
        place_resid(it, h, core)

        def part(c):
            r = pl.multiple_of(c * chunk, chunk)
            grad[h, pl.ds(r, chunk), :] = jnp.dot(
                turned[core, pl.ds(r, chunk), :], masked[core], preferred_element_type=F32
            )

        loop(0, CHUNKS, part)

    def gradient_mate(it, h):
        arrived(it, h, "wm")
        place_resid(it, h, 1 - core)
        for c in range(CHUNKS):
            part = pl.ds(c * chunk, chunk)
            grad[h, part, :] += jnp.dot(turned[1 - core, part, :], masked[1 - core], preferred_element_type=F32)

            def body(b, r):
                code, scale = encode(grad[h, pl.ds(r, BLOCK), pl.ds(0, BLOCK)])
                grad_code[it, h, pl.ds(r, BLOCK), :] = code
                grad_scale[it, h, c, pl.ds(b, 1), :] = scale

            over_blocks(c, body)
            start(it, h, f"gc{c}", f"gs{c}")

    def smooth(it, h):
        arrived(it, h, "hl", "hr")
        first = jnp.where(g == 0, 0.0, 1.0)
        last = jnp.where(g == 3, 0.0, 1.0)
        before, after = jnp.maximum(g - 1, 0), jnp.minimum(g + 1, 3)
        w = wide[it, h]
        high = w.astype(BF16)
        split[0] = high
        split[1] = (w - high.astype(F32)).astype(BF16)
        for c in range(CHUNKS):

            def body(b, r):
                high = split[0, pl.ds(r, 2 * BLOCK), :]
                window = jnp.concatenate([high, high, split[1, pl.ds(r, 2 * BLOCK), :]], axis=0)
                near = jnp.dot(stencil[c * chunk_blocks + b], window, preferred_element_type=F32)
                old = first * decode(coded[it, h, before, pl.ds(r, BLOCK), :], scales[it, h, before, c, pl.ds(b, 1), :])
                new = last * decode(coded[it, h, after, pl.ds(r, BLOCK), :], scales[it, h, after, c, pl.ds(b, 1), :])
                base[h, pl.ds(r, BLOCK), :] = (
                    wide[it, h, pl.ds(HALO + r, BLOCK), :] * keep_rows[pl.ds(r, BLOCK), :]
                    + near
                    + time_rows[pl.ds(r, BLOCK), :] * (old + new)
                )

            over_blocks(c, body)

    def store(h):
        return pltpu.make_async_copy(
            result.at[h], out_hbm.at[0, :, pl.ds(h * BLOCK, BLOCK)], store_sem.at[h]
        )

    def update(it, h):
        for c in range(CHUNKS):
            arrived(it, h, f"gc{c}", f"gs{c}")

            def body(b, r):
                theirs = decode(grad_code_in[it, h, pl.ds(r, BLOCK), :], grad_scale_in[it, h, c, pl.ds(b, 1), :])
                new = base[h, pl.ds(r, BLOCK), :] - step_rows[pl.ds(r, BLOCK), :] * (
                    grad[h, pl.ds(r, BLOCK), pl.ds(BLOCK, BLOCK)] + theirs
                )
                if it == ITERS - 1:
                    result[h, pl.ds(r, BLOCK), :] = new
                else:
                    wide[it + 1, h, pl.ds(HALO + r, BLOCK), :] = new

            over_blocks(c, body)
            if it < ITERS - 1:
                encode_state(it + 1, h, c)
                start(it + 1, h, f"pc{c}", f"ps{c}")
        if it < ITERS - 1:
            start(it + 1, h, *local, *rims)
        else:
            store(h).start()

    turn = pltpu.make_async_remote_copy(
        src_ref=turned.at[core],
        dst_ref=turned.at[core],
        send_sem=turn_sem.at[0],
        recv_sem=turn_sem.at[1],
        device_id=mate,
        device_id_type=MESH,
    )

    def prepare():
        for load in loads[HALVES:]:
            load.wait()

        def arc(a):
            r = pl.multiple_of(a * rows, rows)
            turned[core, :, pl.ds(r, rows)] = panels[pl.ds(r, rows), :].T

        loop(0, arcs, arc)
        by_row = weights[...].astype(F32).T
        for a in range(arcs):
            weight_rows[a * rows : (a + 1) * rows, :] = jnp.broadcast_to(by_row[:, a : a + 1], (rows, BLOCK))

        count = neighbours.shape[0]
        here = s * cols + lax.broadcasted_iota(jnp.int32, (count, cols), 1)
        offset = neighbours[...] - here + HALO
        offset = jnp.where(offset < 0, offset + total, offset)
        offset = jnp.where(offset >= total, offset - total, offset)
        step = RELAX / diag[...]
        near = coef[...]
        own = jnp.sum(near, axis=0, keepdims=True)
        time = coupling[...].reshape(1, cols)
        table = jnp.concatenate(
            [offset.astype(F32), near * step, step, 1.0 - step * (own + 2.0 * time), step * time, jnp.zeros_like(step)],
            axis=0,
        )
        columns[...] = table.T

        def body(b):
            r = pl.multiple_of(b * BLOCK, BLOCK)
            part = columns[pl.ds(r, BLOCK), :]
            place = (
                lax.broadcasted_iota(jnp.int32, (BLOCK, 2 * BLOCK), 1)
                - lax.broadcasted_iota(jnp.int32, (BLOCK, 2 * BLOCK), 0)
            ).astype(F32)
            band = jnp.zeros((BLOCK, 2 * BLOCK), F32)
            for n in range(count):
                band = band + jnp.where(place == part[:, n : n + 1], part[:, count + n : count + n + 1], 0.0)
            high = band.astype(BF16)
            low = (band - high.astype(F32)).astype(BF16)
            stencil[b, :, pl.ds(0, 2 * BLOCK)] = high
            stencil[b, :, pl.ds(2 * BLOCK, 2 * BLOCK)] = low
            stencil[b, :, pl.ds(4 * BLOCK, 2 * BLOCK)] = high
            for k, where in enumerate((step_rows, keep_rows, time_rows)):
                where[pl.ds(r, BLOCK), :] = jnp.broadcast_to(
                    part[:, 2 * count + k : 2 * count + k + 1], (BLOCK, BLOCK)
                )

        loop(0, blocks, body)

    def settle(it, h):
        sent(it, h, *names)
        for d in PEERS:
            reduce_copy(it, h, d).wait_send()
            gather_copy(it, h, d).wait_send()

    for h in range(HALVES):
        loads[h].wait()
        for c in range(CHUNKS):
            encode_state(0, h, c)
        if h == 0:
            pl.semaphore_wait(barrier, 19)
            start(0, 0, *across)
        start(0, h, *local)
    prepare()
    chip_months(0, 0)
    sent(0, 0, *across)
    start(0, 0, *rims)
    start(0, 1, *across, *rims)
    for it in range(ITERS):
        far_arrive(it, 0)
        far_predict(it, 0)
        reduce_start(it, 0)
        if it == 0:
            turn.start()
        else:
            settle(it - 1, 0)
        chip_months(it, 1)
        smooth(it, 0)
        far_arrive(it, 1)
        far_predict(it, 1)
        reduce_start(it, 1)
        reduce_plane(it, 0)
        smooth(it, 1)
        weigh(it, 0)
        if it == 0:
            turn.wait()
        else:
            settle(it - 1, 1)
        reduce_plane(it, 1)
        gradient_here(it, 0)
        weigh(it, 1)
        gradient_mate(it, 0)
        gradient_here(it, 1)
        gradient_mate(it, 1)
        update(it, 0)
        if it < ITERS - 1:
            chip_months(it + 1, 0)
            update(it, 1)
    settle(ITERS - 1, 0)
    update(ITERS - 1, 1)
    settle(ITERS - 1, 1)
    for h in range(HALVES):
        store(h).wait()


def on_device(panels, observations, data_weights, arc_month, fields, diag_scale, smooth_coef, neighbours, time_coupling):
    arcs, rows, cols = panels.shape
    samples = fields.shape[2]
    total = cols * lax.axis_size("mascon")
    every = arcs * rows
    piece = every // 16
    stages = (ITERS, HALVES)
    anywhere = pl.BlockSpec(memory_space=pl.ANY)
    return pl.pallas_call(
        functools.partial(kernel, (cols, arcs, rows, total)),
        out_shape=jax.ShapeDtypeStruct(fields.shape, F32),
        in_specs=[pl.BlockSpec(memory_space=pltpu.SMEM)] + [anywhere] * 8,
        out_specs=anywhere,
        scratch_shapes=[
            pltpu.VMEM((every, cols), BF16),
            pltpu.VMEM((every, samples), BF16),
            pltpu.VMEM(data_weights.shape, BF16),
            pltpu.VMEM(diag_scale.shape, F32),
            pltpu.VMEM(smooth_coef.shape, F32),
            pltpu.VMEM(neighbours.shape, jnp.int32),
            pltpu.VMEM(time_coupling.shape, F32),
            pltpu.VMEM((HALVES, cols, BLOCK), F32),
            pltpu.VMEM((2, cols, every), BF16),
            pltpu.VMEM(stages + (cols + 2 * HALO, BLOCK), F32),
            pltpu.VMEM(stages + (4, cols, BLOCK), I16),
            pltpu.VMEM(stages + (4, CHUNKS, 8, BLOCK), F32),
            pltpu.VMEM((HALVES, cols, 4 * BLOCK), BF16),
            pltpu.VMEM((4, every, BLOCK), F32),
            pltpu.VMEM(stages + (every, BLOCK), F32),
            pltpu.VMEM(stages + (16, piece, BLOCK), F32),
            pltpu.VMEM(stages + (piece, BLOCK), F32),
            pltpu.VMEM(stages + (piece, BLOCK), F32),
            pltpu.VMEM(stages + (2, every, BLOCK), BF16),
            pltpu.VMEM((2, every, 2 * BLOCK), BF16),
            pltpu.VMEM((HALVES, cols, 2 * BLOCK), F32),
            pltpu.VMEM(stages + (cols, BLOCK), I16),
            pltpu.VMEM(stages + (CHUNKS, 8, BLOCK), F32),
            pltpu.VMEM(stages + (cols, BLOCK), I16),
            pltpu.VMEM(stages + (CHUNKS, 8, BLOCK), F32),
            pltpu.VMEM((HALVES, cols, BLOCK), F32),
            pltpu.VMEM((every, BLOCK), F32),
            pltpu.VMEM((cols // BLOCK, BLOCK, 6 * BLOCK), BF16),
            pltpu.VMEM((cols, BLOCK), F32),
            pltpu.VMEM((cols, BLOCK), F32),
            pltpu.VMEM((cols, BLOCK), F32),
            pltpu.VMEM((cols, 16), F32),
            pltpu.VMEM((2, cols + 2 * HALO, BLOCK), BF16),
            pltpu.SemaphoreType.DMA((HALVES + 7,)),
            pltpu.SemaphoreType.DMA((HALVES,)),
            pltpu.SemaphoreType.DMA((ITERS * HALVES * 2, 16)),
            pltpu.SemaphoreType.DMA((ITERS * HALVES * 2, 16)),
            pltpu.SemaphoreType.DMA((ITERS * HALVES, 18)),
            pltpu.SemaphoreType.DMA((ITERS * HALVES, 18)),
            pltpu.SemaphoreType.DMA((2,)),
        ],
        compiler_params=pltpu.CompilerParams(
            collective_id=0, has_side_effects=True, vmem_limit_bytes=56 * 1024 * 1024
        ),
        cost_estimate=pl.CostEstimate(flops=6 * 10**9, bytes_accessed=8 * 10**6, transcendentals=0),
    )(
        arc_month,
        panels.reshape(every, cols),
        observations.reshape(every, samples),
        data_weights,
        fields,
        diag_scale,
        smooth_coef,
        neighbours,
        time_coupling,
    )


def solution(mesh):
    return jax.shard_map(
        on_device,
        mesh=mesh,
        in_specs=(
            P("month", None, "mascon"),
            P("month", None, None),
            P("month", None),
            P(),
            P("month", "mascon", None),
            P("month", "mascon"),
            P(None, "mascon"),
            P(None, "mascon"),
            P("mascon"),
        ),
        out_specs=P("month", "mascon", None),
        check_vma=False,
    )
```

profile of v0, /device:TPU:0, one launch (start us, length us, event | category | flops | bytes accessed | tf_op | source)
XLA Modules:
  0.0 116.6 jit_solution(3415536816328770531)
XLA Ops:
  0.0 114.1 %shard_map.91 = f32[1,1280,256]{2,1,0:T(8,128)} custom-call(s32[32]{0:T(128)} %arc_month.1, bf16[1024,1280]{1,0:T(8,128)(2,1)} %bitcast.2, bf16[1024,256]{1,0:T(8,128)(2,1)} %bitcast.3, bf16[8,128]{1,0:T(8,128)(2,1)} %weights_hbm.1, f32[1,1280,256]{2,1,0:T(8,128)} %fields_hbm.1, f32[1,1280]{1,0:T(1,128)} %diag_hbm.1, f32[6,1280]{1,0:T(8,128)} %coef_hbm.1, ...), custom_call_target="tpu_custom_call" | custom-call | flops 6000000000 | bytes 8000000 | tf_op jit(solution)/shard_map/pallas_call | solution.py:528
  114.1 2.5 %copy.11 = f32[1,1280,256]{2,1,0:T(8,128)} copy(f32[1,1280,256]{2,1,0:T(8,128)} %shard_map.91) | data formatting | bytes 2621440
where the time goes:
time: 117 us
  Pallas kernels  114 us (97%)
  local copies, waits for them, and re-layouts  2.46 us (2%)
    pallas_call x1, Pallas kernels, on_device(): pl.pallas_call(functools.partial(kernel, (cols, arcs, rows, total)), out_...  114 us
    unnamed x1, local copies, waits for them, and re-layouts  2.46 us

commit v1 on v0

--- a/solution.py
+++ b/solution.py
@@ -21,19 +21,29 @@
 F32, BF16, I16 = jnp.float32, jnp.bfloat16, jnp.int16
 
 
-def encode(x):
-    top = jnp.maximum(jnp.max(jnp.abs(x), axis=0, keepdims=True), 1e-30)
-    code = jnp.round(x * (LEVELS / top)).astype(jnp.int32).astype(I16)
-    return code, top * (1.0 / LEVELS)
-
-
-def decode(code, scale):
-    return code.astype(jnp.int32).astype(F32) * scale
+FINE = 256.0
+MARK = 16
+
+
+def level_code(top):
+    return jnp.ceil(jnp.log2(jnp.maximum(top, 1e-30)) * FINE) + 1.0
+
+
+def level(code):
+    return jnp.exp2(code * (1.0 / FINE))
+
+
+def to_code(x):
+    return x.astype(jnp.int32).astype(I16)
+
+
+def to_float(code):
+    return code.astype(jnp.int32).astype(F32)
 
 
 def kernel(
     shape,
-    arc_month,
+    arc_hbm,
     panels_hbm,
     obs_hbm,
     weights_hbm,
@@ -43,6 +53,7 @@
     neighbours_hbm,
     coupling_hbm,
     out_hbm,
+    arc_month,
     panels,
     obs,
     weights,
@@ -54,7 +65,10 @@
     turned,
     wide,
     coded,
-    scales,
+    rim,
+    tops,
+    gains,
+    units,
     states,
     every_month,
     track,
@@ -65,9 +79,7 @@
     masked,
     grad,
     grad_code,
-    grad_scale,
     grad_code_in,
-    grad_scale_in,
     base,
     weight_rows,
     stencil,
@@ -109,9 +121,11 @@
     def device(p):
         return (g, p * 2 + x_lo)
 
-    across = ("pc0", "ps0", "pc1", "ps1")
-    local = ("mc", "ms")
+    across = ("pc0", "pc1")
+    local = ("mc",)
     rims = ("hl", "hr")
+
+    tops[...] = jnp.ones_like(tops)
 
     barrier = pltpu.get_barrier_semaphore()
 
@@ -130,6 +144,7 @@
         for h in range(HALVES)
     ]
     pairs = (
+        (arc_hbm, arc_month),
         (panels_hbm, panels),
         (neighbours_hbm, neighbours),
         (coef_hbm, coef),
@@ -142,35 +157,26 @@
     for load in loads:
         load.start()
 
-    names = ("pc0", "pc1", "ps0", "ps1", "fc0", "fc1", "fs0", "fs1", "gc0", "gc1", "gs0", "gs1")
-    names += ("mc", "ms", "hl", "hr", "xl", "wm")
-    targets = (pair, pair, pair, pair, mate, mate, mate, mate, pair, pair, pair, pair)
-    targets += (mate, mate, left, right, beside, mate)
+    names = ("pc0", "pc1", "fc0", "fc1", "gc0", "gc1", "mc", "hl", "hr", "xl", "wm")
+    targets = (pair, pair, mate, mate, pair, pair, mate, left, right, beside, mate)
+    coded_chunk = chunk + MARK
+    marks = (pl.ds(0, MARK), pl.ds(MARK + cols, MARK))
 
     def copy(it, h, name):
-        w = wide.at[it, h]
         c = int(name[2]) if len(name) == 3 else 0
-        part = pl.ds(c * chunk, chunk)
+        part = pl.ds(c * coded_chunk, coded_chunk)
         if name[:2] == "pc":
             src = dst = coded.at[it, h, g, part]
-        elif name[:2] == "ps":
-            src = dst = scales.at[it, h, g, c]
         elif name[:2] == "fc":
             src = dst = coded.at[it, h, pair_month, part]
-        elif name[:2] == "fs":
-            src = dst = scales.at[it, h, pair_month, c]
         elif name[:2] == "gc":
             src, dst = grad_code.at[it, h, part], grad_code_in.at[it, h, part]
-        elif name[:2] == "gs":
-            src, dst = grad_scale.at[it, h, c], grad_scale_in.at[it, h, c]
         elif name == "mc":
             src = dst = coded.at[it, h, g]
-        elif name == "ms":
-            src = dst = scales.at[it, h, g]
         elif name == "hl":
-            src, dst = w.at[pl.ds(HALO, HALO)], w.at[pl.ds(HALO + cols, HALO)]
+            src, dst = coded.at[it, h, g, pl.ds(0, HALO + MARK)], rim.at[it, h, 1]
         elif name == "hr":
-            src, dst = w.at[pl.ds(cols, HALO)], w.at[pl.ds(0, HALO)]
+            src, dst = coded.at[it, h, g, pl.ds(MARK + cols - HALO, HALO + MARK)], rim.at[it, h, 0]
         elif name == "xl":
             src, dst = lane_sum.at[it, h], lane_got.at[it, h]
         else:
@@ -212,8 +218,7 @@
         )
 
     def reduce_copy(it, h, d):
-        first = pl.multiple_of(peer(d) * piece, piece)
-        return plane(it, h, 0, d, track.at[it, h, pl.ds(first, piece)], partial.at[it, h, d])
+        return plane(it, h, 0, d, track.at[it, h, peer(d)], partial.at[it, h, d])
 
     def gather_copy(it, h, d):
         first = pl.multiple_of(q * piece, piece)
@@ -233,20 +238,42 @@
     def lane(month):
         return pl.multiple_of((((month // 2) + hi) % 2 * 2 + month % 2) * BLOCK, BLOCK)
 
+    def data(r, size=BLOCK):
+        return pl.ds(pl.multiple_of(MARK + r, MARK), size)
+
+    def encode(c, read, ref):
+        def peak(b, r):
+            tops[pl.ds(b, 1), :] = jnp.max(jnp.abs(read(r)), axis=0, keepdims=True)
+
+        def put(b, r):
+            ref[data(r), :] = to_code(jnp.round(read(r) * gains[pl.ds(b, 1), :]))
+
+        over_blocks(c, peak)
+        code = level_code(tops[...])
+        ref[marks[c], :] = to_code(code)
+        gains[...] = LEVELS / level(code)
+        over_blocks(c, put)
+
+    def set_units(i, c, ref):
+        units[i] = level(to_float(ref[marks[c], :])) * (1.0 / LEVELS)
+
+    def decode(i, ref, b, r):
+        return to_float(ref[data(r), :]) * units[i, pl.ds(b, 1), :]
+
     def encode_state(it, h, c):
+        encode(c, lambda r: wide[it, h, pl.ds(HALO + r, BLOCK), :], coded.at[it, h, g])
+
         def body(b, r):
-            x = wide[it, h, pl.ds(HALO + r, BLOCK), :]
-            code, scale = encode(x)
-            coded[it, h, g, pl.ds(r, BLOCK), :] = code
-            scales[it, h, g, c, pl.ds(b, 1), :] = scale
-            states[h, pl.ds(r, BLOCK), pl.ds(lane(g), BLOCK)] = x.astype(BF16)
+            states[h, pl.ds(r, BLOCK), pl.ds(lane(g), BLOCK)] = wide[it, h, pl.ds(HALO + r, BLOCK), :].astype(BF16)
 
         over_blocks(c, body)
 
     def unpack(it, h, month, c):
+        ref = coded.at[it, h, month]
+        set_units(0, c, ref)
+
         def body(b, r):
-            x = decode(coded[it, h, month, pl.ds(r, BLOCK), :], scales[it, h, month, c, pl.ds(b, 1), :])
-            states[h, pl.ds(r, BLOCK), pl.ds(lane(month), BLOCK)] = x.astype(BF16)
+            states[h, pl.ds(r, BLOCK), pl.ds(lane(month), BLOCK)] = decode(0, ref, b, r).astype(BF16)
 
         over_blocks(c, body)
 
@@ -264,20 +291,20 @@
         loop(0, 2, part)
 
     def chip_months(it, h):
-        arrived(it, h, "mc", "ms")
+        arrived(it, h, "mc")
         for c in range(CHUNKS):
             unpack(it, h, mate_month, c)
         predict(h, 0)
 
     def far_arrive(it, h):
         for c in range(CHUNKS):
-            arrived(it, h, f"pc{c}", f"ps{c}")
-            start(it, h, f"fc{c}", f"fs{c}")
+            arrived(it, h, f"pc{c}")
+            start(it, h, f"fc{c}")
             unpack(it, h, pair_month, c)
 
     def far_predict(it, h):
         for c in range(CHUNKS):
-            arrived(it, h, f"fc{c}", f"fs{c}")
+            arrived(it, h, f"fc{c}")
             unpack(it, h, far_month, c)
         predict(h, 1)
 
@@ -285,7 +312,12 @@
             month = arc_month[g * arcs + a]
             r = pl.multiple_of(a * rows, rows)
             place = (month // 2 + hi) % 2 * 2 + month % 2
-            track[it, h, pl.ds(r, rows), :] = every_month[place, pl.ds(r, rows), :]
+            for u in range(rows // piece):
+                sums = every_month[place, pl.ds(r + u * piece, piece), :]
+                code = level_code(jnp.max(jnp.abs(sums), axis=0, keepdims=True))
+                p = a * (rows // piece) + u
+                track[it, h, p, pl.ds(0, piece), :] = to_code(jnp.round(sums * (LEVELS / level(code))))
+                track[it, h, p, pl.ds(piece, MARK), :] = to_code(jnp.broadcast_to(code, (MARK, BLOCK)))
 
         loop(0, arcs, choose)
 
@@ -294,12 +326,15 @@
             reduce_copy(it, h, d).start()
 
     def reduce_plane(it, h):
+        def value(code):
+            both = to_float(code)
+            return both[:piece] * (level(both[piece : piece + 1]) * (1.0 / LEVELS))
+
         def add(d, acc):
             reduce_copy(it, h, d).wait_recv()
-            return acc + partial[it, h, d]
-
-        own = track[it, h, pl.ds(pl.multiple_of(q * piece, piece), piece), :]
-        lane_sum[it, h] = lax.fori_loop(1, 16, add, own)
+            return acc + value(partial[it, h, d])
+
+        lane_sum[it, h] = lax.fori_loop(1, 16, add, value(track[it, h, q]))
         start(it, h, "xl")
 
     def weigh(it, h):
@@ -341,31 +376,33 @@
             part = pl.ds(c * chunk, chunk)
             grad[h, part, :] += jnp.dot(turned[1 - core, part, :], masked[1 - core], preferred_element_type=F32)
 
-            def body(b, r):
-                code, scale = encode(grad[h, pl.ds(r, BLOCK), pl.ds(0, BLOCK)])
-                grad_code[it, h, pl.ds(r, BLOCK), :] = code
-                grad_scale[it, h, c, pl.ds(b, 1), :] = scale
-
-            over_blocks(c, body)
-            start(it, h, f"gc{c}", f"gs{c}")
+            encode(c, lambda r: grad[h, pl.ds(r, BLOCK), pl.ds(0, BLOCK)], grad_code.at[it, h])
+            start(it, h, f"gc{c}")
 
     def smooth(it, h):
         arrived(it, h, "hl", "hr")
         first = jnp.where(g == 0, 0.0, 1.0)
         last = jnp.where(g == 3, 0.0, 1.0)
         before, after = jnp.maximum(g - 1, 0), jnp.minimum(g + 1, 3)
+        rims_in = to_float(rim[it, h, 0]), to_float(rim[it, h, 1])
+        unit = level(rims_in[0][HALO + chunk_blocks - 1 : HALO + chunk_blocks]) * (1.0 / LEVELS)
+        wide[it, h, pl.ds(0, HALO), :] = rims_in[0][:HALO] * unit
+        unit = level(rims_in[1][:1]) * (1.0 / LEVELS)
+        wide[it, h, pl.ds(HALO + cols, HALO), :] = rims_in[1][MARK:] * unit
         w = wide[it, h]
         high = w.astype(BF16)
         split[0] = high
         split[1] = (w - high.astype(F32)).astype(BF16)
         for c in range(CHUNKS):
+            set_units(0, c, coded.at[it, h, before])
+            set_units(1, c, coded.at[it, h, after])
 
             def body(b, r):
                 high = split[0, pl.ds(r, 2 * BLOCK), :]
                 window = jnp.concatenate([high, high, split[1, pl.ds(r, 2 * BLOCK), :]], axis=0)
                 near = jnp.dot(stencil[c * chunk_blocks + b], window, preferred_element_type=F32)
-                old = first * decode(coded[it, h, before, pl.ds(r, BLOCK), :], scales[it, h, before, c, pl.ds(b, 1), :])
-                new = last * decode(coded[it, h, after, pl.ds(r, BLOCK), :], scales[it, h, after, c, pl.ds(b, 1), :])
+                old = first * decode(0, coded.at[it, h, before], b, r)
+                new = last * decode(1, coded.at[it, h, after], b, r)
                 base[h, pl.ds(r, BLOCK), :] = (
                     wide[it, h, pl.ds(HALO + r, BLOCK), :] * keep_rows[pl.ds(r, BLOCK), :]
                     + near
@@ -374,17 +411,19 @@
 
             over_blocks(c, body)
 
-    def store(h):
+    def store(h, c):
+        part = pl.ds(c * chunk, chunk)
         return pltpu.make_async_copy(
-            result.at[h], out_hbm.at[0, :, pl.ds(h * BLOCK, BLOCK)], store_sem.at[h]
+            result.at[h, part], out_hbm.at[0, part, pl.ds(h * BLOCK, BLOCK)], store_sem.at[h, c]
         )
 
     def update(it, h):
         for c in range(CHUNKS):
-            arrived(it, h, f"gc{c}", f"gs{c}")
+            arrived(it, h, f"gc{c}")
+            set_units(0, c, grad_code_in.at[it, h])
 
             def body(b, r):
-                theirs = decode(grad_code_in[it, h, pl.ds(r, BLOCK), :], grad_scale_in[it, h, c, pl.ds(b, 1), :])
+                theirs = decode(0, grad_code_in.at[it, h], b, r)
                 new = base[h, pl.ds(r, BLOCK), :] - step_rows[pl.ds(r, BLOCK), :] * (
                     grad[h, pl.ds(r, BLOCK), pl.ds(BLOCK, BLOCK)] + theirs
                 )
@@ -396,11 +435,11 @@
             over_blocks(c, body)
             if it < ITERS - 1:
                 encode_state(it + 1, h, c)
-                start(it + 1, h, f"pc{c}", f"ps{c}")
+                start(it + 1, h, f"pc{c}")
+            else:
+                store(h, c).start()
         if it < ITERS - 1:
             start(it + 1, h, *local, *rims)
-        else:
-            store(h).start()
 
     turn = pltpu.make_async_remote_copy(
         src_ref=turned.at[core],
@@ -494,8 +533,8 @@
         far_predict(it, 1)
         reduce_start(it, 1)
         reduce_plane(it, 0)
+        weigh(it, 0)
         smooth(it, 1)
-        weigh(it, 0)
         if it == 0:
             turn.wait()
         else:
@@ -514,7 +553,8 @@
     update(ITERS - 1, 1)
     settle(ITERS - 1, 1)
     for h in range(HALVES):
-        store(h).wait()
+        for c in range(CHUNKS):
+            store(h, c).wait()
 
 
 def on_device(panels, observations, data_weights, arc_month, fields, diag_scale, smooth_coef, neighbours, time_coupling):
@@ -528,9 +568,10 @@
     return pl.pallas_call(
         functools.partial(kernel, (cols, arcs, rows, total)),
         out_shape=jax.ShapeDtypeStruct(fields.shape, F32),
-        in_specs=[pl.BlockSpec(memory_space=pltpu.SMEM)] + [anywhere] * 8,
+        in_specs=[anywhere] * 9,
         out_specs=anywhere,
         scratch_shapes=[
+            pltpu.SMEM(arc_month.shape, jnp.int32),
             pltpu.VMEM((every, cols), BF16),
             pltpu.VMEM((every, samples), BF16),
             pltpu.VMEM(data_weights.shape, BF16),
@@ -541,21 +582,22 @@
             pltpu.VMEM((HALVES, cols, BLOCK), F32),
             pltpu.VMEM((2, cols, every), BF16),
             pltpu.VMEM(stages + (cols + 2 * HALO, BLOCK), F32),
-            pltpu.VMEM(stages + (4, cols, BLOCK), I16),
-            pltpu.VMEM(stages + (4, CHUNKS, 8, BLOCK), F32),
+            pltpu.VMEM(stages + (4, cols + CHUNKS * MARK, BLOCK), I16),
+            pltpu.VMEM(stages + (2, HALO + MARK, BLOCK), I16),
+            pltpu.VMEM((MARK, BLOCK), F32),
+            pltpu.VMEM((MARK, BLOCK), F32),
+            pltpu.VMEM((2, MARK, BLOCK), F32),
             pltpu.VMEM((HALVES, cols, 4 * BLOCK), BF16),
             pltpu.VMEM((4, every, BLOCK), F32),
-            pltpu.VMEM(stages + (every, BLOCK), F32),
-            pltpu.VMEM(stages + (16, piece, BLOCK), F32),
+            pltpu.VMEM(stages + (16, piece + MARK, BLOCK), I16),
+            pltpu.VMEM(stages + (16, piece + MARK, BLOCK), I16),
             pltpu.VMEM(stages + (piece, BLOCK), F32),
             pltpu.VMEM(stages + (piece, BLOCK), F32),
             pltpu.VMEM(stages + (2, every, BLOCK), BF16),
             pltpu.VMEM((2, every, 2 * BLOCK), BF16),
             pltpu.VMEM((HALVES, cols, 2 * BLOCK), F32),
-            pltpu.VMEM(stages + (cols, BLOCK), I16),
-            pltpu.VMEM(stages + (CHUNKS, 8, BLOCK), F32),
-            pltpu.VMEM(stages + (cols, BLOCK), I16),
-            pltpu.VMEM(stages + (CHUNKS, 8, BLOCK), F32),
+            pltpu.VMEM(stages + (cols + CHUNKS * MARK, BLOCK), I16),
+            pltpu.VMEM(stages + (cols + CHUNKS * MARK, BLOCK), I16),
             pltpu.VMEM((HALVES, cols, BLOCK), F32),
             pltpu.VMEM((every, BLOCK), F32),
             pltpu.VMEM((cols // BLOCK, BLOCK, 6 * BLOCK), BF16),
@@ -564,12 +606,12 @@
             pltpu.VMEM((cols, BLOCK), F32),
             pltpu.VMEM((cols, 16), F32),
             pltpu.VMEM((2, cols + 2 * HALO, BLOCK), BF16),
-            pltpu.SemaphoreType.DMA((HALVES + 7,)),
-            pltpu.SemaphoreType.DMA((HALVES,)),
+            pltpu.SemaphoreType.DMA((HALVES + 8,)),
+            pltpu.SemaphoreType.DMA((HALVES, CHUNKS)),
             pltpu.SemaphoreType.DMA((ITERS * HALVES * 2, 16)),
             pltpu.SemaphoreType.DMA((ITERS * HALVES * 2, 16)),
-            pltpu.SemaphoreType.DMA((ITERS * HALVES, 18)),
-            pltpu.SemaphoreType.DMA((ITERS * HALVES, 18)),
+            pltpu.SemaphoreType.DMA((ITERS * HALVES, 11)),
+            pltpu.SemaphoreType.DMA((ITERS * HALVES, 11)),
             pltpu.SemaphoreType.DMA((2,)),
         ],
         compiler_params=pltpu.CompilerParams(

time: 117 us -> 112 us (0.957)
  Pallas kernels: 114 us -> 109 us
    pallas_call x1, Pallas kernels: 114 us -> 109 us  [on_device(): pl.pallas_call(functools.partial(kernel, (cols, arcs, rows, total)), out_...]
where the time goes in v1:
time: 112 us; the launch traced here: 111 us
  Pallas kernels  109 us (97%)
  local copies, waits for them, and re-layouts  2.46 us (2%)
    pallas_call x1, Pallas kernels, on_device(): pl.pallas_call(functools.partial(kernel, (cols, arcs, rows, total)), out_...  109 us
    unnamed x1, local copies, waits for them, and re-layouts  2.46 us

profile of v1, /device:TPU:0, one launch (start us, length us, event | category | flops | bytes accessed | tf_op | source)
XLA Modules:
  0.0 111.0 jit_solution(15887602674351652718)
XLA Ops:
  0.0 108.5 %shard_map.91 = f32[1,1280,256]{2,1,0:T(8,128)} custom-call(s32[32]{0:T(128)} %arc_hbm.1, bf16[1024,1280]{1,0:T(8,128)(2,1)} %bitcast.2, bf16[1024,256]{1,0:T(8,128)(2,1)} %bitcast.3, bf16[8,128]{1,0:T(8,128)(2,1)} %weights_hbm.1, f32[1,1280,256]{2,1,0:T(8,128)} %fields_hbm.1, f32[1,1280]{1,0:T(1,128)} %diag_hbm.1, f32[6,1280]{1,0:T(8,128)} %coef_hbm.1, ...), custom_call_target="tpu_custom_call" | custom-call | flops 6000000000 | bytes 8000000 | tf_op jit(solution)/shard_map/pallas_call | solution.py:568
  108.5 2.5 %copy.11 = f32[1,1280,256]{2,1,0:T(8,128)} copy(f32[1,1280,256]{2,1,0:T(8,128)} %shard_map.91) | data formatting | bytes 2621440

commit v2 on v1

--- a/solution.py
+++ b/solution.py
@@ -369,7 +369,7 @@
 
         loop(0, CHUNKS, part)
 
-    def gradient_mate(it, h):
+    def gradient_mate(it, h, go):
         arrived(it, h, "wm")
         place_resid(it, h, 1 - core)
         for c in range(CHUNKS):
@@ -377,7 +377,8 @@
             grad[h, part, :] += jnp.dot(turned[1 - core, part, :], masked[1 - core], preferred_element_type=F32)
 
             encode(c, lambda r: grad[h, pl.ds(r, BLOCK), pl.ds(0, BLOCK)], grad_code.at[it, h])
-            start(it, h, f"gc{c}")
+            if go:
+                start(it, h, f"gc{c}")
 
     def smooth(it, h):
         arrived(it, h, "hl", "hr")
@@ -417,8 +418,9 @@
             result.at[h, part], out_hbm.at[0, part, pl.ds(h * BLOCK, BLOCK)], store_sem.at[h, c]
         )
 
-    def update(it, h):
-        for c in range(CHUNKS):
+    def update(it, h, chunks=range(CHUNKS)):
+        more = it < ITERS - 1
+        for c in chunks:
             arrived(it, h, f"gc{c}")
             set_units(0, c, grad_code_in.at[it, h])
 
@@ -433,13 +435,16 @@
                     wide[it + 1, h, pl.ds(HALO + r, BLOCK), :] = new
 
             over_blocks(c, body)
-            if it < ITERS - 1:
+            if more:
                 encode_state(it + 1, h, c)
-                start(it + 1, h, f"pc{c}")
+                if h == 0 or c == 0:
+                    start(it + 1, h, f"pc{c}")
             else:
                 store(h, c).start()
-        if it < ITERS - 1:
-            start(it + 1, h, *local, *rims)
+        if more and CHUNKS - 1 in chunks:
+            start(it + 1, h, *local)
+            if h == 0:
+                start(it + 1, h, *rims)
 
     turn = pltpu.make_async_remote_copy(
         src_ref=turned.at[core],
@@ -519,36 +524,53 @@
     sent(0, 0, *across)
     start(0, 0, *rims)
     start(0, 1, *across, *rims)
-    for it in range(ITERS):
+    far_arrive(0, 0)
+    far_predict(0, 0)
+    reduce_start(0, 0)
+    turn.start()
+    chip_months(0, 1)
+    smooth(0, 0)
+    far_arrive(0, 1)
+    far_predict(0, 1)
+    reduce_start(0, 1)
+    reduce_plane(0, 0)
+    weigh(0, 0)
+    smooth(0, 1)
+    turn.wait()
+    reduce_plane(0, 1)
+    gradient_here(0, 0)
+    weigh(0, 1)
+    gradient_mate(0, 0, True)
+    gradient_here(0, 1)
+    for it in range(1, ITERS):
+        update(it - 1, 0, (0,))
+        gradient_mate(it - 1, 1, False)
+        update(it - 1, 0, (1,))
+        start(it - 1, 1, "gc0", "gc1")
+        chip_months(it, 0)
         far_arrive(it, 0)
         far_predict(it, 0)
         reduce_start(it, 0)
-        if it == 0:
-            turn.start()
-        else:
-            settle(it - 1, 0)
+        smooth(it, 0)
+        update(it - 1, 1)
+        reduce_plane(it, 0)
+        start(it, 1, "pc1", *rims)
+        settle(it - 1, 0)
         chip_months(it, 1)
-        smooth(it, 0)
+        weigh(it, 0)
         far_arrive(it, 1)
         far_predict(it, 1)
         reduce_start(it, 1)
-        reduce_plane(it, 0)
-        weigh(it, 0)
+        gradient_here(it, 0)
+        gradient_mate(it, 0, False)
+        reduce_plane(it, 1)
+        start(it, 0, "gc0", "gc1")
         smooth(it, 1)
-        if it == 0:
-            turn.wait()
-        else:
-            settle(it - 1, 1)
-        reduce_plane(it, 1)
-        gradient_here(it, 0)
+        settle(it - 1, 1)
         weigh(it, 1)
-        gradient_mate(it, 0)
         gradient_here(it, 1)
-        gradient_mate(it, 1)
-        update(it, 0)
-        if it < ITERS - 1:
-            chip_months(it + 1, 0)
-            update(it, 1)
+    gradient_mate(ITERS - 1, 1, True)
+    update(ITERS - 1, 0)
     settle(ITERS - 1, 0)
     update(ITERS - 1, 1)
     settle(ITERS - 1, 1)

time: 112 us -> 112 us (level)
  no operation moved by 1% of the time
where the time goes in v2:
time: 112 us; the launch traced here: 111 us
  Pallas kernels  108 us (96%)
  local copies, waits for them, and re-layouts  2.46 us (2%)
    pallas_call x1, Pallas kernels, on_device(): pl.pallas_call(functools.partial(kernel, (cols, arcs, rows, total)), out_...  108 us
    unnamed x1, local copies, waits for them, and re-layouts  2.46 us

profile of v2, /device:TPU:0, one launch (start us, length us, event | category | flops | bytes accessed | tf_op | source)
XLA Modules:
  0.0 110.9 jit_solution(4319087263070680886)
XLA Ops:
  0.0 108.4 %shard_map.91 = f32[1,1280,256]{2,1,0:T(8,128)} custom-call(s32[32]{0:T(128)} %arc_hbm.1, bf16[1024,1280]{1,0:T(8,128)(2,1)} %bitcast.2, bf16[1024,256]{1,0:T(8,128)(2,1)} %bitcast.3, bf16[8,128]{1,0:T(8,128)(2,1)} %weights_hbm.1, f32[1,1280,256]{2,1,0:T(8,128)} %fields_hbm.1, f32[1,1280]{1,0:T(1,128)} %diag_hbm.1, f32[6,1280]{1,0:T(8,128)} %coef_hbm.1, ...), custom_call_target="tpu_custom_call" | custom-call | flops 6000000000 | bytes 8000000 | tf_op jit(solution)/shard_map/pallas_call | solution.py:590
  108.4 2.5 %copy.11 = f32[1,1280,256]{2,1,0:T(8,128)} copy(f32[1,1280,256]{2,1,0:T(8,128)} %shard_map.91) | data formatting | bytes 2621440
